TPU v7x, 256 devices: a whole 4x4x8 slice. The times are simulated.
256 devices in a mesh: row: 8 (over x, z_hi), col: 32 (over y, z_lo, core).
Axes of the slice: x: 4, y: 4, z: 8 (z_hi: 2, z_lo: 4; z = z_hi * 4 + z_lo), core: 2. Of those that a mesh axis runs over, the one named last changes fastest.
Arguments:
- pair_rep: bfloat16 [1792, 1792, 128], P('row', 'col'), may hold values from -6 to 6
- norm_in: float32 [2, 128], replicated, may hold values from 0.1 to 1.9
- proj_weight: bfloat16 [2, 128, 512], replicated, may hold values from -0.5 to 0.5
- gate_weight: bfloat16 [2, 128, 128], replicated, may hold values from -0.5 to 0.5
- norm_out: float32 [2, 128], replicated, may hold values from 0.1 to 1.9
- out_weight: bfloat16 [2, 128, 128], replicated, may hold values from -0.5 to 0.5
Outputs:
- outgoing: bfloat16 [256, 1792, 128], P(('row', 'col'))
- incoming: bfloat16 [256, 1792, 128], P(('row', 'col'))
All inputs are finite; a program needn't handle non-finite values.
Results may differ from a plain program's by a relative error of at most 0.019.
Values may be sent and summed in bfloat16 or wider, within the bound.
A program may use at most 128 MiB of HBM per device.

v0:
```python
import jax
import jax.numpy as jnp
from jax import lax
from jax.sharding import PartitionSpec as P


def layer_norm(values, scales, along):
    values = values.astype(jnp.float32)
    average = jnp.mean(values, axis=along, keepdims=True)
    centered = values - average
    spread = jnp.mean(centered * centered, axis=along, keepdims=True)
    return centered * lax.rsqrt(spread + 1e-05) * scales


def gated(block, scales, weights):
    normed = layer_norm(block, scales, 2).astype(jnp.bfloat16)
    projected = jnp.einsum("rkc,cg->grk", normed, weights, preferred_element_type=jnp.float32)
    hidden = weights.shape[1] // 2
    return (jax.nn.sigmoid(projected[:hidden]) * projected[hidden:]).astype(jnp.bfloat16)


def finish(mixed, band_pairs, scales_in, w_gating, scales_out, w_output):
    settled = layer_norm(mixed, scales_out[None, :, None], 1).astype(jnp.bfloat16)
    linear = jnp.einsum("ahn,hc->anc", settled, w_output, preferred_element_type=jnp.float32)
    normed_rows = layer_norm(band_pairs, scales_in, 2).astype(jnp.bfloat16)
    gating = jax.nn.sigmoid(
        jnp.einsum("anc,ce->ane", normed_rows, w_gating, preferred_element_type=jnp.float32)
    )
    return (gating * linear).astype(jnp.bfloat16)


def shards(pair_rep, norm_in, proj_weight, gate_weight, norm_out, out_weight):
    stride = pair_rep.shape[0] // lax.axis_size("col")
    hidden = proj_weight.shape[2] // 4
    band_rows = pair_rep[::stride]
    band_cols = pair_rep[:, ::stride]
    gathered_rows = lax.all_to_all(band_rows, "col", split_axis=0, concat_axis=1, tiled=True)
    weights = proj_weight[0]
    first_out = gated(band_rows, norm_in[0], weights[:, : 2 * hidden])
    second_out = gated(pair_rep, norm_in[0], weights[:, 2 * hidden :])
    second_split, first_split = (
        lax.all_to_all(second_out, "col", split_axis=0, concat_axis=2, tiled=True),
        lax.all_to_all(first_out, "col", split_axis=0, concat_axis=2, tiled=True),
    )
    terms_out = jnp.einsum(
        "qik,qjk->iqj",
        lax.all_gather(first_split, "row", axis=1, tiled=True),
        second_split,
        preferred_element_type=jnp.float32,
    ).astype(jnp.bfloat16)
    mixed_out = lax.all_to_all(
        lax.all_to_all(terms_out, "row", split_axis=0, concat_axis=2, tiled=True),
        "col",
        split_axis=0,
        concat_axis=1,
        tiled=True,
    )
    result_out = finish(
        mixed_out, gathered_rows, norm_in[0], gate_weight[0], norm_out[0], out_weight[0]
    )
    weights = proj_weight[1]
    first_in = gated(band_cols, norm_in[1], weights[:, : 2 * hidden])
    second_in = gated(pair_rep, norm_in[1], weights[:, 2 * hidden :])
    second_group, first_group = (
        lax.all_to_all(second_in, "row", split_axis=0, concat_axis=1, tiled=True),
        lax.all_to_all(first_in, "row", split_axis=0, concat_axis=1, tiled=True),
    )
    terms_in = jnp.einsum(
        "qki,qkj->iqj",
        lax.all_gather(first_group, "col", axis=2, tiled=True),
        second_group,
        preferred_element_type=jnp.float32,
    ).astype(jnp.bfloat16)
    mixed_in = lax.all_to_all(
        lax.all_to_all(terms_in, "row", split_axis=0, concat_axis=1, tiled=True),
        "col",
        split_axis=0,
        concat_axis=2,
        tiled=True,
    )
    result_in = finish(
        mixed_in, gathered_rows, norm_in[1], gate_weight[1], norm_out[1], out_weight[1]
    )
    return (result_out, result_in)


def solution(mesh):
    in_specs = (P("row", "col", None), P(), P(), P(), P(), P())
    out_specs = (P(("row", "col"), None, None), P(("row", "col"), None, None))
    return jax.shard_map(shards, mesh=mesh, in_specs=in_specs, out_specs=out_specs, check_vma=False)
```

profile of v0, /device:TPU:1, one launch (start us, length us, event | category | flops | bytes accessed | tf_op | source)
XLA Modules:
  0.0 544.0 jit_solution(2343847521892289611)
XLA Ops:
  8.0 1.0 slice_bitcast_fusion
  9.0 1.4 convert_reduce_fusion.2
  10.4 1.6 fusion.42
  12.0 1.7 convolution_bitcast_fusion.3
  13.8 1.0 fusion.49
  14.8 3.4 copy.65
  18.2 3.9 reshape.628
  22.2 25.7 %all_to_all.135 = bf16[32,2,3584]{2,1,0:T(2,128)(2,1)} all-to-all(bf16[32,2,3584]{2,1,0:T(2,128)(2,1)} %reshape.628), channel_id=1, replica_groups=mesh['row'=8,'col'=32] {'col'}, dimensions={0} | all-to-all | bytes 917504 | tf_op jit(solution)/shard_map/all_to_all | solution.py:43
  47.9 4.0 reshape.629
  51.9 2.9 copy.66
  54.9 3.2 all_to_all.107
  58.4 3.0 slice.99
  61.4 1.3 convert_reduce_fusion.1
  62.7 1.6 fusion.39
  64.3 1.7 convolution_bitcast_fusion.2
  66.0 1.0 fusion.45
  67.0 2.4 copy.74
  69.4 29.8 %all_to_all.136 = bf16[128,224,8]{1,2,0:T(8,128)(2,1)S(1)} all-to-all(bf16[128,224,8]{1,2,0:T(8,128)(2,1)} %copy.74), channel_id=1, replica_groups=mesh['row'=8,'col'=32] {'row'}, dimensions={0} | all-to-all | bytes 917504 | tf_op jit(solution)/shard_map/all_to_all | solution.py:66
  99.2 1.1 copy.75
  100.3 2.5 all_to_all.120
  103.6 5.2 all-to-all-start
  108.8 1.7 convert_reduce_fusion
  110.6 3.7 fusion.6
  114.3 4.7 convolution_bitcast_fusion.1
  119.0 2.9 fusion.11
  121.9 7.1 %copy.63 = bf16[128,224,56]{1,2,0:T(8,128)(2,1)} copy(bf16[128,224,56]{0,2,1:T(8,128)(2,1)} %fusion.11) | data formatting | bytes 6422528 | tf_op jit(solution)/shard_map/convert_element_type | solution.py:19
  129.0 33.9 %all-to-all-done = bf16[32,56,128]{2,1,0:T(8,128)(2,1)} async-done(((bf16[32,56,128]{2,1,0:T(8,128)(2,1)}), bf16[32,56,128]{2,1,0:T(8,128)(2,1)}, u32[]{:S(2)}, u32[]{:S(2)}) %all-to-all-start) | async-done | bytes 458784 | tf_op jit(solution)/shard_map/all_to_all | solution.py:37
  162.9 5.3 all-to-all-start.1
  168.2 4.7 convolution_bitcast_fusion
  172.8 1.7 fusion.7
  174.6 6.9 %copy.72 = bf16[128,224,56]{1,2,0:T(8,128)(2,1)} copy(bf16[128,224,56]{0,2,1:T(8,128)(2,1)S(1)} %fusion.7) | data formatting | bytes 6422528 | tf_op jit(solution)/shard_map/convert_element_type | solution.py:19
  181.4 105.1 %all-to-all-done.1 = bf16[128,224,56]{1,2,0:T(8,128)(2,1)} async-done(((bf16[128,224,56]{1,2,0:T(8,128)(2,1)}), bf16[128,224,56]{1,2,0:T(8,128)(2,1)}, u32[]{:S(2)}, u32[]{:S(2)}) %all-to-all-start.1) | async-done | bytes 3211296 | tf_op jit(solution)/shard_map/all_to_all | solution.py:42
  286.5 4.5 all-to-all-start.5
  291.1 4.1 copy.64
  295.1 4.5 fusion.34
  299.7 1.1 copy.68
  300.8 66.9 %all-to-all-done.5 = bf16[128,224,56]{1,2,0:T(8,128)(2,1)} async-done(((bf16[128,224,56]{1,2,0:T(8,128)(2,1)}), bf16[128,224,56]{1,2,0:T(8,128)(2,1)}, u32[]{:S(2)}, u32[]{:S(2)}) %all-to-all-start.5) | async-done | bytes 3211296 | tf_op jit(solution)/shard_map/all_to_all | solution.py:65
  367.7 4.4 all-to-all-start.3
  372.1 1.3 convert_reduce_fusion.3
  373.6 1.1 convert_element_type.213
  375.2 5.9 %copy.73 = bf16[16,8,224,56]{2,1,3,0:T(8,128)(2,1)} copy(bf16[16,8,224,56]{2,3,0,1:T(8,128)(2,1)} %bitcast.28) | data formatting | bytes 6422528 | tf_op jit(solution)/shard_map/all_to_all | solution.py:65
  381.1 6.4 %all_to_all.116 = bf16[16,1792,56]{1,2,0:T(8,128)(2,1)S(1)} reshape(bf16[16,8,224,56]{2,1,3,0:T(8,128)(2,1)} %copy.73) | data formatting | bytes 6422528 | tf_op jit(solution)/shard_map/all_to_all | solution.py:65
  387.5 4.4 all-to-all-done.3
  391.9 1.1 copy.69
  393.0 1.1 copy.81
  394.1 2.5 reshape.627
  396.7 68.3 %all-to-all-start.4 = ((bf16[32,4,1792]{2,1,0:T(4,128)(2,1)}), bf16[32,4,1792]{2,1,0:T(4,128)(2,1)}, u32[]{:S(2)}, u32[]{:S(2)}) async-start(bf16[32,4,1792]{2,1,0:T(4,128)(2,1)} %reshape.627), calls=%async_computation.4 | async-start | bytes 917504 | tf_op jit(solution)/shard_map/all_to_all | solution.py:51
  465.0 10.5 %fusion.33 = bf16[256,16,56]{0,2,1:T(8,128)(2,1)} fusion(bf16[16,1792,56]{1,2,0:T(8,128)(2,1)S(1)} %all_to_all.116, bf16[16,1792,256]{1,2,0:T(8,128)(2,1)} %all-gather.5.cloned.1.call-done), kind=kOutput, calls=%fused_computation.47 | convolution fusion | flops 822312960 | bytes 18350080 | tf_op jit(solution)/shard_map/qki,qkj->iqj/dot_general | solution.py:68
  475.5 2.0 copy.76
  477.4 2.6 reshape.630
  480.4 9.7 %all-to-all-start.7 = ((bf16[8,2,14336]{2,1,0:T(2,128)(2,1)}), bf16[8,2,14336]{2,1,0:T(2,128)(2,1)S(1)}, u32[]{:S(2)}, u32[]{:S(2)}) async-start(bf16[8,2,14336]{2,1,0:T(2,128)(2,1)} %reshape.630), calls=%async_computation.7 | async-start | bytes 917504 | tf_op jit(solution)/shard_map/all_to_all | solution.py:75
  490.2 1.6 multiply_convert_fusion.1
  491.8 1.3 fusion.28
  493.1 1.4 fusion.25
  494.5 1.1 reshape.619
  495.5 7.4 %all-to-all-done.7 = bf16[8,2,14336]{2,1,0:T(2,128)(2,1)S(1)} async-done(((bf16[8,2,14336]{2,1,0:T(2,128)(2,1)}), bf16[8,2,14336]{2,1,0:T(2,128)(2,1)S(1)}, u32[]{:S(2)}, u32[]{:S(2)}) %all-to-all-start.7) | async-done | bytes 458784 | tf_op jit(solution)/shard_map/all_to_all | solution.py:75
  502.9 1.9 reshape.631
  505.1 1.1 copy.78
  506.2 12.4 %all-to-all-start.8 = ((bf16[32,128,56]{1,2,0:T(8,128)(2,1)}), bf16[32,128,56]{1,2,0:T(8,128)(2,1)S(1)}, u32[]{:S(2)}, u32[]{:S(2)}) async-start(bf16[32,128,56]{1,2,0:T(8,128)(2,1)} %copy.78), calls=%async_computation.8 | async-start | bytes 917504 | tf_op jit(solution)/shard_map/all_to_all | solution.py:74
  518.6 1.2 convert_reduce_fusion.4
  519.8 1.3 multiply_reduce_fusion
  521.2 2.3 fusion.32
  523.5 10.5 %all-to-all-done.8 = bf16[32,128,56]{1,2,0:T(8,128)(2,1)S(1)} async-done(((bf16[32,128,56]{1,2,0:T(8,128)(2,1)}), bf16[32,128,56]{1,2,0:T(8,128)(2,1)S(1)}, u32[]{:S(2)}, u32[]{:S(2)}) %all-to-all-start.8) | async-done | bytes 458784 | tf_op jit(solution)/shard_map/all_to_all | solution.py:74
  535.2 1.4 fusion.31
  (45 shorter events, 4.6 us)
Async XLA Ops:
  7.2 288.0 %all-gather.3.cloned.1.call-start = ((), (), s32[]{:S(2)}) async-start(), calls=%async_computation.9 | async-start | bytes 4128768 | tf_op jit(solution)/shard_map/all_gather | solution.py:47
  9.0 3.1 copy-start.2
  9.0 55.4 %copy-start.3 = (bf16[128,512]{1,0:T(8,128)(2,1)}, bf16[128,512]{1,0:T(8,128)(2,1)S(1)}, u32[]{:S(2)}) copy-start(bf16[128,512]{1,0:T(8,128)(2,1)S(1)} %get-tuple-element.4) | copy-start | bytes 393220
  13.8 44.6 %copy-start = (bf16[224,56,128]{2,1,0:T(8,128)(2,1)S(1)}, bf16[224,56,128]{2,1,0:T(8,128)(2,1)}, u32[]{:S(2)}) copy-start(bf16[224,56,128]{2,1,0:T(8,128)(2,1)} %param.6) | copy-start | bytes 9633796
  58.1 406.9 %all-gather.5.cloned.1.call-start = ((), (), s32[]{:S(2)}) async-start(), calls=%async_computation.10 | async-start | bytes 15138816 | tf_op jit(solution)/shard_map/all_gather | solution.py:70
  103.6 59.3 %all-to-all-start = ((bf16[32,56,128]{2,1,0:T(8,128)(2,1)}), bf16[32,56,128]{2,1,0:T(8,128)(2,1)}, u32[]{:S(2)}, u32[]{:S(2)}) async-start(bf16[32,56,128]{2,1,0:T(8,128)(2,1)} %slice.80), calls=%async_computation | async-start | bytes 917504 | tf_op jit(solution)/shard_map/all_to_all | solution.py:37
  162.9 123.6 %all-to-all-start.1 = ((bf16[128,224,56]{1,2,0:T(8,128)(2,1)}), bf16[128,224,56]{1,2,0:T(8,128)(2,1)}, u32[]{:S(2)}, u32[]{:S(2)}) async-start(bf16[128,224,56]{1,2,0:T(8,128)(2,1)} %copy.63), calls=%async_computation.1 | async-start | bytes 7340032 | tf_op jit(solution)/shard_map/all_to_all | solution.py:42
  286.5 81.2 %all-to-all-start.5 = ((bf16[128,224,56]{1,2,0:T(8,128)(2,1)}), bf16[128,224,56]{1,2,0:T(8,128)(2,1)}, u32[]{:S(2)}, u32[]{:S(2)}) async-start(bf16[128,224,56]{1,2,0:T(8,128)(2,1)} %copy.72), calls=%async_computation.5 | async-start | bytes 7340032 | tf_op jit(solution)/shard_map/all_to_all | solution.py:65
  295.1 77.0 %copy-start.5 = (f32[2,128]{1,0:T(2,128)S(1)}, f32[2,128]{1,0:T(2,128)}, u32[]{:S(2)}) copy-start(f32[2,128]{1,0:T(2,128)} %param.10) | copy-start | bytes 3076
  367.7 24.2 %all-to-all-start.3 = ((bf16[256,4,224]{2,1,0:T(4,128)(2,1)}), bf16[256,4,224]{2,1,0:T(4,128)(2,1)}, u32[]{:S(2)}, u32[]{:S(2)}) async-start(bf16[256,4,224]{2,1,0:T(4,128)(2,1)} %copy.68), calls=%async_computation.3 | async-start | bytes 1048576 | tf_op jit(solution)/shard_map/all_to_all | solution.py:52
  396.7 83.8 %all-to-all-start.4 = ((bf16[32,4,1792]{2,1,0:T(4,128)(2,1)}), bf16[32,4,1792]{2,1,0:T(4,128)(2,1)}, u32[]{:S(2)}, u32[]{:S(2)}) async-start(bf16[32,4,1792]{2,1,0:T(4,128)(2,1)} %reshape.627), calls=%async_computation.4 | async-start | bytes 917504 | tf_op jit(solution)/shard_map/all_to_all | solution.py:51
  465.0 26.8 %copy-start.6 = (bf16[2,128,128]{2,1,0:T(8,128)(2,1)S(1)}, bf16[2,128,128]{2,1,0:T(8,128)(2,1)}, u32[]{:S(2)}) copy-start(bf16[2,128,128]{2,1,0:T(8,128)(2,1)} %param.9) | copy-start | bytes 196612
  480.4 22.5 %all-to-all-start.7 = ((bf16[8,2,14336]{2,1,0:T(2,128)(2,1)}), bf16[8,2,14336]{2,1,0:T(2,128)(2,1)S(1)}, u32[]{:S(2)}, u32[]{:S(2)}) async-start(bf16[8,2,14336]{2,1,0:T(2,128)(2,1)} %reshape.630), calls=%async_computation.7 | async-start | bytes 917504 | tf_op jit(solution)/shard_map/all_to_all | solution.py:75
  493.1 28.1 %copy-start.4 = (bf16[2,128,128]{2,1,0:T(8,128)(2,1)S(1)}, bf16[2,128,128]{2,1,0:T(8,128)(2,1)}, u32[]{:S(2)}) copy-start(bf16[2,128,128]{2,1,0:T(8,128)(2,1)} %param.11) | copy-start | bytes 196612
  506.2 29.0 %copy-start.1 = (f32[1792,128]{1,0:T(8,128)S(1)}, f32[1792,128]{1,0:T(8,128)}, u32[]{:S(2)}) copy-start(f32[1792,128]{1,0:T(8,128)} %fusion.25) | copy-start | bytes 2752516
  506.2 27.8 %all-to-all-start.8 = ((bf16[32,128,56]{1,2,0:T(8,128)(2,1)}), bf16[32,128,56]{1,2,0:T(8,128)(2,1)S(1)}, u32[]{:S(2)}, u32[]{:S(2)}) async-start(bf16[32,128,56]{1,2,0:T(8,128)(2,1)} %copy.78), calls=%async_computation.8 | async-start | bytes 917504 | tf_op jit(solution)/shard_map/all_to_all | solution.py:74
Sparse Core Ops, SparseCore 0:
  58.2 101.2 all-gather.2
  161.3 277.2 all-gather.4
where the time goes:
time: 553 us; the launch traced here: 544 us
  waiting for transfers between devices  229 us (41%)
  starting transfers between devices  110 us (20%)
  local copies, waits for them, and re-layouts  74.5 us (13%)
  blocking collectives  55.6 us (10%)
  matrix products  34.2 us (6%)
  other arithmetic  26.2 us (5%)
  between operations  14.9 us (3%)
    all_to_all x1, waiting for transfers between devices, shards(): lax.all_to_all(second_out, 'col', split_axis=0, concat_axis=2, tiled=True)  105 us
    all_to_all x1, starting transfers between devices, shards(): lax.all_to_all(lax.all_to_all(terms_out, 'row', split_axis=0, concat_axis...  68.3 us
    all_to_all x1, waiting for transfers between devices, shards(): lax.all_to_all(second_in, 'row', split_axis=0, concat_axis=1, tiled=True)  66.9 us
    all_to_all x1, waiting for transfers between devices, shards(): lax.all_to_all(band_rows, 'col', split_axis=0, concat_axis=1, tiled=True)  33.9 us
    all_to_all x1, blocking collectives, shards(): lax.all_to_all(first_in, 'row', split_axis=0, concat_axis=1, tiled=True)  29.8 us
    all_to_all x1, blocking collectives, shards(): lax.all_to_all(first_out, 'col', split_axis=0, concat_axis=2, tiled=True)  25.7 us
    convert_element_type x4, local copies, waits for them, and re-layouts, gated(): (jax.nn.sigmoid(projected[:hidden]) * projected[hidden:]).astype(jnp.bflo...  19.8 us
    dot_general x4, matrix products, gated(): jnp.einsum('rkc,cg->grk', normed, weights, preferred_element_type=jnp.flo...  12.7 us
  transfers between devices with their start and end apart: 9, of which 7 were waited for; matrix products, arithmetic and copies ran while one was open for 17% of the time, Pallas kernels for 0%

commit v1 on v0

v1 whole, which is shorter than its diff:
```python
import jax
import jax.numpy as jnp
from jax import lax
from jax.experimental import pallas as pl
from jax.experimental.pallas import tpu as pltpu
from jax.sharding import PartitionSpec as P

MESH = pl.DeviceIdType.MESH
BF = jnp.bfloat16
F32 = jnp.float32

ROWS = 224
COLS = 56
BAND = 32
BCOL = 8
CHUNK = 14
NCH = COLS // CHUNK
EPS = 1e-05


def gate_value(projected):
    gate, value = projected[:128], projected[128:]
    return (0.5 * value) * (1.0 + jnp.tanh(0.5 * gate))


def sigmoid(x):
    return 0.5 + 0.5 * jnp.tanh(0.5 * x)


def unit_norm(x, axis):
    mean = jnp.mean(x, axis=axis, keepdims=True)
    cent = x - mean
    var = jnp.mean(cent * cent, axis=axis, keepdims=True)
    return cent * lax.rsqrt(var + EPS)


def nt(a, b):
    return lax.dot_general(a, b, (((1,), (1,)), ((), ())), preferred_element_type=F32)


def tn(a, b):
    return lax.dot_general(a, b, (((0,), (0,)), ((), ())), preferred_element_type=F32)


def kernel(pair, norm_in, w_t, gate_w, norm_out, out_w, out0, out1,
           xhat, send0, send1, recv0, recv1, f0s, f0r, f1s, f1r, lhs0, lhs1,
           rhs0, rhs1, tmp, part0, rs0, part1, rs1, zsend, zrecv,
           fin0s, fin0r, fin1s, fin1r, grow, g0, g1,
           a2a_s, a2a_r, f_s, f_r, zh_s, zh_r, x_s, x_r, zl_s, zl_r,
           row_s, row_r, rs0_s, rs0_r, rs1_s, rs1_r, rz_s, rz_r,
           fin_s, fin_r, loc):
    r = lax.axis_index("row")
    c = lax.axis_index("col")
    x, zh = r // 2, r % 2
    y, zl, core = c // 8, (c // 2) % 4, c % 2
    yc = y * 2 + core

    def dev(x_, zh_, y_, zl_, core_):
        return (x_ * 2 + zh_, y_ * 8 + zl_ * 2 + core_)

    def dev_yc(o):
        return dev(x, zh, (y + o // 2) % 4, zl, (core + o) % 2)

    def dst_yc(o):
        return ((y + o // 2) % 4) * 2 + (core + o) % 2

    def slot_yc(y_, core_):
        return ((y - y_ + 4) % 4) * 2 + (core - core_ + 2) % 2

    barrier = pltpu.get_barrier_semaphore()

    def greet_col(i, _):
        pl.semaphore_signal(barrier, inc=1, device_id=(r, (c + i) % 32), device_id_type=MESH)
        return 0

    def peer64(i):
        s_, o = (r + i // 8) % 8, i % 8
        return s_, o

    def greet_64(i, _):
        s_, o = peer64(i)
        pl.semaphore_signal(
            barrier, inc=1,
            device_id=(s_, ((y + o // 2) % 4) * 8 + zl * 2 + (core + o) % 2),
            device_id_type=MESH)
        return 0

    lax.fori_loop(1, 32, greet_col, 0)
    lax.fori_loop(8, 64, greet_64, 0)

    def remote(src, dst, ssem, rsem, device):
        return pltpu.make_async_remote_copy(
            src_ref=src, dst_ref=dst, send_sem=ssem, recv_sem=rsem,
            device_id=device, device_id_type=MESH)

    def norm_body(i, _):
        v = pair[pl.ds(i * 4, 4)].astype(F32)
        xhat[pl.ds(i * 4 * COLS, 4 * COLS), :] = unit_norm(v, 2).reshape(4 * COLS, 128)
        return 0

    lax.fori_loop(0, ROWS // 4, norm_body, 0)

    gain0 = norm_in[0:1, :]
    gain1 = norm_in[1:2, :]

    def band_row(u):
        tl = ((u // 2) % 4) * 8 + (u // 8) * 2 + u % 2
        v = xhat[pl.ds(pl.multiple_of(tl * 7 * COLS, 8), COLS), :] * gain0
        return jnp.concatenate([v, jnp.zeros((8, 128), F32)], axis=0)

    def first0_body(i, _):
        rows = jnp.concatenate(
            [band_row(2 * i), band_row(2 * i + 16), band_row(2 * i + 1), band_row(2 * i + 17)],
            axis=0).astype(BF)
        v = gate_value(nt(w_t[0, 0:256, :], rows)).astype(BF)
        f0s[:, 2 * i] = v[:, :128].reshape(8, 16, 128)
        f0s[:, 2 * i + 1] = v[:, 128:].reshape(8, 16, 128)
        return 0

    lax.fori_loop(0, 8, first0_body, 0)

    def column(k, gain):
        v = xhat[pl.ds(k, ROWS, stride=COLS), :] * gain
        return jnp.concatenate([v, jnp.zeros((32, 128), F32)], axis=0).astype(BF)

    def first1_body(b, _):
        v = gate_value(nt(w_t[1, 0:256, :], column(b * 7, gain1))).astype(BF)
        f1s[:, b] = v.reshape(8, 16, 256)
        return 0

    lax.fori_loop(0, BCOL, first1_body, 0)

    pl.semaphore_wait(barrier, 31 + 56)

    def a2a_start(src, dst, ssem, rsem):
        def go(o, _):
            remote(src(dst_yc(o)), dst(o), ssem, rsem, dev_yc(o)).start()
            return 0
        lax.fori_loop(1, 8, go, 0)

    def a2a_wait(src7, dst7, ssem, rsem):
        d = remote(src7, dst7, ssem, rsem, dev_yc(1))
        d.wait_send()
        d.wait_recv()

    a2a_start(lambda d: f0s.at[d], lambda o: f0r.at[o], f_s.at[0], f_r.at[0])
    f0r[0] = f0s[yc]
    a2a_start(lambda d: f1s.at[d], lambda o: f1r.at[o], f_s.at[1], f_r.at[1])
    f1r[0] = f1s[yc]

    def rows_start(i, _):
        cc = (c + i) % 32
        remote(pair.at[cc * 7], grow.at[c], row_s, row_r, (r, cc)).start()
        return 0

    def second(w, gain, send, recv, d):
        for ch in range(NCH):
            def body(k, _):
                v = gate_value(nt(w_t[w, 256:512, :], column(k, gain))).astype(BF)
                send[:, k] = v.reshape(8, 16, 256)
                return 0
            lax.fori_loop(ch * CHUNK, (ch + 1) * CHUNK, body, 0)
            part = pl.ds(ch * CHUNK, CHUNK)
            a2a_start(lambda q: send.at[q, part], lambda o: recv.at[o, part],
                      a2a_s.at[d, ch], a2a_r.at[d, ch])
            recv[0, part] = send[yc, part]

    def second_wait(send, recv, d):
        for ch in range(NCH):
            part = pl.ds(ch * CHUNK, CHUNK)
            a2a_wait(send.at[pl.ds(0, 7), part], recv.at[pl.ds(1, 7), part],
                     a2a_s.at[d, ch], a2a_r.at[d, ch])

    second(0, gain0, send0, recv0, 0)

    a2a_wait(f0s.at[pl.ds(0, 7)], f0r.at[pl.ds(1, 7)], f_s.at[0], f_r.at[0])
    low = lax.broadcasted_iota(jnp.int32, (16 * 16, 128), 1) < 64
    for y_ in range(4):
        a = f0r[slot_yc(y_, 0)].astype(F32).reshape(256, 128)
        b = f0r[slot_yc(y_, 1)].astype(F32).reshape(256, 128)
        tmp[0, 0:256, :] = jnp.where(low, a, pltpu.roll(b, 64, 1))
        tmp[0, 256:512, :] = jnp.where(low, pltpu.roll(a, 64, 1), b)
        for h in range(16):
            lhs0[r, h, :, y_ * 128:(y_ + 1) * 128] = tmp[0, pl.ds(h, 32, stride=16), :].astype(BF)

    zh_copy = remote(lhs0.at[r], lhs0.at[r], zh_s, zh_r, dev(x, 1 - zh, y, zl, core))
    zh_copy.start()
    other = x * 2 + 1 - zh
    x_first = [remote(lhs0.at[r], lhs0.at[r], x_s.at[0, i], x_r.at[0, i],
                      dev((x + i) % 4, zh, y, zl, core)) for i in range(1, 4)]
    for d in x_first:
        d.start()

    a2a_wait(f1s.at[pl.ds(0, 7)], f1r.at[pl.ds(1, 7)], f_s.at[1], f_r.at[1])
    for y_ in range(4):
        for half in range(2):
            lanes = slice(half * 128, half * 128 + 128)
            for cc in range(2):
                tmp[half, cc * 128:cc * 128 + 128, :] = (
                    f1r[slot_yc(y_, cc), :, :, lanes].astype(F32).reshape(128, 128))
            for h in range(16):
                lhs1[zl, h, y_ * 16:(y_ + 1) * 16, lanes] = (
                    tmp[half, pl.ds(h, 16, stride=16), :].astype(BF))
    zl_copies = [remote(lhs1.at[zl], lhs1.at[zl], zl_s.at[i], zl_r.at[i],
                        dev(x, zh, y, (zl + i) % 4, core)) for i in range(1, 4)]
    for d in zl_copies:
        d.start()

    second(1, gain1, send1, recv1, 1)

    lax.fori_loop(1, 32, rows_start, 0)
    grow[c] = pair[c * 7]

    zh_copy.wait_recv()
    x_second = [remote(lhs0.at[other], lhs0.at[other], x_s.at[1, i], x_r.at[1, i],
                       dev((x + i) % 4, zh, y, zl, core)) for i in range(1, 4)]
    for d in x_second:
        d.start()

    def spread(recv, y_):
        def body(i, _):
            for cc in range(2):
                v = recv[slot_yc(y_, cc), pl.ds(i * 8, 8)].astype(F32).reshape(128, 256)
                at = pl.ds(pl.multiple_of(cc * 896 + i * 128, 128), 128)
                tmp[0, at, :] = v[:, :128]
                tmp[1, at, :] = v[:, 128:]
            return 0
        lax.fori_loop(0, 7, body, 0)

    second_wait(send0, recv0, 0)
    pad8 = jnp.zeros((8, 128), F32)
    for y_ in range(4):
        spread(recv0, y_)

        def body(h, _):
            for half in range(2):
                v = jnp.concatenate(
                    [tmp[half, pl.ds(h, 56, stride=16), :], pad8,
                     tmp[half, pl.ds(h + 896, 56, stride=16), :], pad8], axis=0)
                rhs0[h, y_ * 128:(y_ + 1) * 128, half * 128:half * 128 + 128] = v.astype(BF)
            return 0
        lax.fori_loop(0, 16, body, 0)

    for d in x_first + x_second:
        d.wait_recv()

    def product0(h, _):
        a = lhs0[:, h].reshape(256, 512)
        v = jnp.dot(a, rhs0[h], preferred_element_type=F32).astype(F32).reshape(8, 4, 8, 256)
        for q in range(4):
            part0[q, h] = v[:, q].reshape(64, 256).astype(BF)
        return 0

    lax.fori_loop(0, 16, product0, 0)
    rs0_copies = [remote(part0.at[(zl + i) % 4], rs0.at[i - 1], rs0_s.at[i], rs0_r.at[i],
                         dev(x, zh, y, (zl + i) % 4, core)) for i in range(1, 4)]
    for d in rs0_copies:
        d.start()

    second_wait(send1, recv1, 1)
    for y_ in range(4):
        spread(recv1, y_)

        def body(h, _):
            for half in range(2):
                rhs1[h, y_ * 112:(y_ + 1) * 112, half * 128:half * 128 + 128] = (
                    tmp[half, pl.ds(h, 112, stride=16), :].astype(BF))
            return 0
        lax.fori_loop(0, 16, body, 0)
    for d in zl_copies:
        d.wait_recv()

    def product1(h, _):
        a = lhs1[:, h].reshape(256, 256)
        v = nt(a, rhs1[h]).reshape(4, 4, 16, 448)
        for q in range(4):
            part1[q, h] = v[:, q].reshape(64, 448).astype(BF)
        return 0

    lax.fori_loop(0, 16, product1, 0)
    rs1_copies = [remote(part1.at[(x + i) % 4], rs1.at[i - 1], rs1_s.at[i], rs1_r.at[i],
                         dev((x + i) % 4, zh, y, zl, core)) for i in range(1, 4)]
    for d in rs1_copies:
        d.start()

    rows_all = remote(grow.at[pl.ds(0, 31)], grow.at[pl.ds(0, 31)], row_s, row_r, (r, (c + 1) % 32))
    rows_all.wait_send()
    rows_all.wait_recv()

    def gates(i, _):
        v = unit_norm(grow[pl.ds(i * 4, 4)].astype(F32), 2).reshape(4 * COLS, 128)
        at = pl.ds(pl.multiple_of(i * 4 * COLS, 8), 4 * COLS)
        g0[at, :] = sigmoid(jnp.dot((v * gain0).astype(BF), gate_w[0], preferred_element_type=F32))
        g1[at, :] = sigmoid(jnp.dot((v * gain1).astype(BF), gate_w[1], preferred_element_type=F32))
        return 0

    lax.fori_loop(0, 8, gates, 0)

    for d in rs0_copies:
        d.wait_recv()

    def sum0(h, _):
        v = part0[zl, h].astype(F32)
        for i in range(3):
            v = v + rs0[i, h].astype(F32)
        at = pl.ds(pl.multiple_of(h * 64, 64), 64)
        tmp[0, at, :] = v[:, :128]
        tmp[1, at, :] = v[:, 128:]
        return 0

    lax.fori_loop(0, 16, sum0, 0)

    def turn0(t, _):
        fin0s[t] = jnp.concatenate(
            [tmp[half, pl.ds(t, 16, stride=64), :] for half in range(2)], axis=1).astype(BF)
        return 0

    lax.fori_loop(0, 64, turn0, 0)
    me64 = r * 8 + yc

    def fin0_start(i, _):
        s_, o = peer64(i)
        q = dst_yc(o)
        remote(fin0s.at[s_ * 8 + q], fin0r.at[me64], fin_s.at[0], fin_r.at[0],
               (s_, (q // 2) * 8 + zl * 2 + q % 2)).start()
        return 0

    lax.fori_loop(1, 64, fin0_start, 0)
    fin0r[me64] = fin0s[me64]

    for d in rs1_copies:
        d.wait_recv()

    def sum1(h, _):
        v = part1[x, h].astype(F32)
        for i in range(3):
            v = v + rs1[i, h].astype(F32)
        v = v.astype(BF)
        zsend[0, h] = v[:32]
        zsend[1, h] = v[32:]
        return 0

    lax.fori_loop(0, 16, sum1, 0)
    rz = remote(zsend.at[1 - zh], zrecv, rz_s, rz_r, dev(x, 1 - zh, y, zl, core))
    rz.start()

    fin0_all = remote(fin0s.at[pl.ds(0, 63)], fin0r.at[pl.ds(0, 63)], fin_s.at[0], fin_r.at[0], dev_yc(1))
    fin0_all.wait_send()
    fin0_all.wait_recv()

    def settle(v, d):
        return (unit_norm(v.astype(F32), 0) * norm_out[d]).astype(BF)

    def finish0(s, _):
        v = fin0r[pl.ds(s * 8, 8)].reshape(128, 256)
        linear = tn(settle(v, 0), out_w[0])[:ROWS]
        at = pl.ds(pl.multiple_of(s * ROWS, 8), ROWS)
        out0[0, pl.ds(pl.multiple_of(s * ROWS, 16), ROWS), :] = (g0[at, :] * linear).astype(BF)
        return 0

    lax.fori_loop(0, 8, finish0, 0)

    rz.wait_recv()

    def sum2(h, _):
        v = zsend[zh, h].astype(F32) + zrecv[h].astype(F32)
        at = pl.ds(pl.multiple_of(h * 32, 32), 32)
        for q in range(3):
            tmp[q // 2, pl.ds(pl.multiple_of((q % 2) * 512 + h * 32, 32), 32), :] = v[:, q * 128:(q + 1) * 128]
        tmp[1, pl.ds(pl.multiple_of(512 + h * 32, 32), 32), :] = jnp.concatenate(
            [v[:, 384:], jnp.zeros((32, 64), F32)], axis=1)
        return 0

    lax.fori_loop(0, 16, sum2, 0)

    def turn1(t, _):
        v = jnp.concatenate(
            [tmp[q // 2, pl.ds((q % 2) * 512 + t, 16, stride=32), :] for q in range(4)], axis=1)
        fin1s[t] = v[:, :448].astype(BF)
        return 0

    lax.fori_loop(0, 32, turn1, 0)

    def fin1_start(i, _):
        cc = (c + i) % 32
        remote(fin1s.at[cc], fin1r.at[c], fin_s.at[1], fin_r.at[1], (r, cc)).start()
        return 0

    lax.fori_loop(1, 32, fin1_start, 0)
    fin1r[c] = fin1s[c]
    fin1_all = remote(fin1s.at[pl.ds(0, 31)], fin1r.at[pl.ds(0, 31)], fin_s.at[1], fin_r.at[1], dev_yc(1))
    fin1_all.wait_send()
    fin1_all.wait_recv()

    for z_ in range(4):
        v = jnp.concatenate(
            [fin1r[y_ * 8 + z_ * 2 + cc] for y_ in range(4) for cc in range(2)], axis=0)
        linear = tn(settle(v, 1), out_w[1])
        for y_ in range(4):
            at = (y_ * 8 + z_ * 2) * COLS
            out1[0, at:at + 112, :] = (
                g1[at:at + 112, :] * linear[y_ * 112:(y_ + 1) * 112]).astype(BF)

    zh_copy.wait_send()
    rz.wait_send()
    for d in x_first + x_second + zl_copies + rs0_copies + rs1_copies:
        d.wait_send()


def shards(pair_rep, norm_in, proj_weight, gate_weight, norm_out, out_weight):
    w_t = jnp.swapaxes(proj_weight, 1, 2)
    vm = pl.BlockSpec(memory_space=pltpu.VMEM)
    dma = pltpu.SemaphoreType.DMA
    V = pltpu.VMEM
    return pl.pallas_call(
        kernel,
        name="triangles",
        out_shape=[jax.ShapeDtypeStruct((1, 1792, 128), BF)] * 2,
        in_specs=[vm] * 6,
        out_specs=[vm] * 2,
        scratch_shapes=[
            V((ROWS * COLS, 128), F32),
            V((8, COLS, 16, 256), BF), V((8, COLS, 16, 256), BF),
            V((8, COLS, 16, 256), BF), V((8, COLS, 16, 256), BF),
            V((8, 16, 16, 128), BF), V((8, 16, 16, 128), BF),
            V((8, 8, 16, 256), BF), V((8, 8, 16, 256), BF),
            V((8, 16, 32, 512), BF), V((4, 16, 64, 256), BF),
            V((16, 512, 256), BF), V((16, 448, 256), BF),
            V((2, 1792, 128), F32),
            V((4, 16, 64, 256), BF), V((3, 16, 64, 256), BF),
            V((4, 16, 64, 448), BF), V((3, 16, 64, 448), BF),
            V((2, 16, 32, 448), BF), V((16, 32, 448), BF),
            V((64, 16, 256), BF), V((64, 16, 256), BF),
            V((32, 16, 448), BF), V((32, 16, 448), BF),
            V((32, COLS, 128), BF), V((1792, 128), F32), V((1792, 128), F32),
            dma((2, NCH)), dma((2, NCH)), dma((2,)), dma((2,)), dma, dma,
            dma((2, 4)), dma((2, 4)), dma((4,)), dma((4,)),
            dma, dma, dma((4,)), dma((4,)), dma((4,)), dma((4,)), dma, dma,
            dma((2,)), dma((2,)), dma,
        ],
        compiler_params=pltpu.CompilerParams(
            collective_id=0, has_side_effects=True, vmem_limit_bytes=60 << 20),
    )(pair_rep, norm_in, w_t, gate_weight, norm_out[:, :, None], out_weight)


def solution(mesh):
    in_specs = (P("row", "col", None), P(), P(), P(), P(), P())
    out_specs = (P(("row", "col"), None, None), P(("row", "col"), None, None))
    return jax.shard_map(shards, mesh=mesh, in_specs=in_specs, out_specs=out_specs, check_vma=False)
```

time: 553 us -> 231 us (0.42); the launches traced: 544 us -> 231 us
  waiting for transfers between devices: 229 us -> 0 us
  Pallas kernels: 0 us -> 223 us
  starting transfers between devices: 110 us -> 0 us
  local copies, waits for them, and re-layouts: 74.5 us -> 6.89 us
  blocking collectives: 55.6 us -> 0 us
  matrix products: 34.2 us -> 0 us
  other arithmetic: 26.2 us -> 0 us
  between operations: 14.9 us -> 0.64 us
    all_to_all x7 -> x0, waiting for transfers between devices: 229 us -> none  [the longest x1 105 us: shards(): lax.all_to_all(second_out, 'col', split_axis=0, concat_axis=2, tiled=True)]
    pallas_call x0 -> x1, Pallas kernels: none -> 223 us  [shards(): pl.pallas_call(kernel, name='triangles', out_shape=[jax.ShapeDtypeStruct(...]
    all_to_all x7 -> x0, starting transfers between devices: 110 us -> none  [the longest x1 68.3 us: shards(): lax.all_to_all(lax.all_to_all(terms_out, 'row', split_axis=0, concat_axis...]
    all_to_all x2 -> x0, blocking collectives: 55.6 us -> none  [the longest x1 29.8 us: shards(): lax.all_to_all(first_in, 'row', split_axis=0, concat_axis=1, tiled=True)]
    dot_general x10 -> x0, matrix products: 34.2 us -> none  [the longest x4 12.7 us: gated(): jnp.einsum('rkc,cg->grk', normed, weights, preferred_element_type=jnp.flo...]
    all_to_all x12 -> x0, local copies, waits for them, and re-layouts: 32.2 us -> none  [the longest x2 12.3 us: shards(): lax.all_to_all(second_in, 'row', split_axis=0, concat_axis=1, tiled=True)]
    convert_element_type x7 -> x0, local copies, waits for them, and re-layouts: 24 us -> none  [the longest x4 19.8 us: gated(): (jax.nn.sigmoid(projected[:hidden]) * projected[hidden:]).astype(jnp.bflo...]
    reduce_sum x12 -> x0, other arithmetic: 16.7 us -> none  [the longest x6 9.36 us: layer_norm(): spread = jnp.mean(centered * centered, axis=along, keepdims=True)]
  transfers between devices with their start and end apart: 9 -> 0, of which waited for: 7 -> 0; matrix products, arithmetic and copies ran while one was open for 17% -> 0% of each run, Pallas kernels for 0% -> 0%
where the time goes in v1:
time: 231 us
  Pallas kernels  223 us (97%)
  local copies, waits for them, and re-layouts  6.89 us (3%)
    pallas_call x1, Pallas kernels, shards(): pl.pallas_call(kernel, name='triangles', out_shape=[jax.ShapeDtypeStruct(...  223 us
    unnamed x3, local copies, waits for them, and re-layouts  5.42 us

profile of v1, /device:TPU:1, one launch (start us, length us, event | category | flops | bytes accessed | tf_op | source)
XLA Modules:
  0.0 230.9 jit_solution(14899601211650198194)
XLA Ops:
  0.6 1.5 copy.10.norm_out
  2.1 1.8 copy.9
  3.9 223.4 %triangles.1 = (bf16[1,1792,128]{2,1,0:T(8,128)(2,1)}, bf16[1,1792,128]{2,1,0:T(8,128)(2,1)}) custom-call(bf16[224,56,128]{2,1,0:T(8,128)(2,1)} %pair.1, f32[2,128]{1,0:T(2,128)} %norm_in.1, bf16[2,512,128]{2,1,0:T(8,128)(2,1)} %bitcast.2, bf16[2,128,128]{2,1,0:T(8,128)(2,1)} %gate_w.1, f32[2,128,1]{2,1,0:T(8,128)} %copy.10.norm_out, bf16[2,128,128]{2,1,0:T(8,128)(2,1)} %out_w.1), custom_call_target="tpu_custom_call" | custom-call | tf_op jit(solution)/shard_map/triangles/pallas_call | solution.py:415
  227.3 1.8 copy.13
  229.1 1.8 copy.14

commit v2 on v0

v2 whole, which is shorter than its diff:
```python
import jax
import jax.numpy as jnp
from jax import lax
from jax.experimental import pallas as pl
from jax.experimental.pallas import tpu as pltpu
from jax.sharding import PartitionSpec as P

MESH = pl.DeviceIdType.MESH
BF = jnp.bfloat16
F32 = jnp.float32

ROWS = 224
COLS = 56
EPS = 1e-05
TILES = 25
CUTS = ((0, 4, 0, 14), (4, 7, 14, 25))
WIDE = 16


def gate_value(projected):
    gate, value = projected[:256], projected[256:]
    return (0.5 * value) * (1.0 + jnp.tanh(0.5 * gate))


def sigmoid(x):
    return 0.5 + 0.5 * jnp.tanh(0.5 * x)


def unit_norm(x, axis):
    mean = jnp.mean(x, axis=axis, keepdims=True)
    cent = x - mean
    var = jnp.mean(cent * cent, axis=axis, keepdims=True)
    return cent * lax.rsqrt(var + EPS)


def nt(a, b):
    return lax.dot_general(a, b, (((1,), (1,)), ((), ())), preferred_element_type=F32)


def tn(a, b):
    return lax.dot_general(a, b, (((0,), (0,)), ((), ())), preferred_element_type=F32)


def lane_of(v):
    return lax.broadcasted_iota(jnp.int32, v.shape, len(v.shape) - 1)


def roll(v, by):
    return pltpu.roll(v, by, len(v.shape) - 1)


def unpack(t0, t1, t2):
    lane = lane_of(t0)
    zero = jnp.zeros_like(t0)
    parts = (t0, roll(jnp.where(lane < 64, t1, t0), 32),
             roll(jnp.where(lane < 32, t2, t1), 64), roll(t2, 96))
    return [jnp.where(lane < 96, p, zero) for p in parts]


def kernel(pair, norm_in, w, gate_w, norm_out, out_w, out0, out1,
           xhat, wb, send0, send1, recv0, recv1, f0s, f0r, f1s, f1r, lhs0, lhs1,
           rhs0, rhs1, tmp, part0, rs0, part1, zrecv, xs, xr,
           fin0s, fin0r, fin1s, fin1r, grow, g0, g1,
           a2a_s, a2a_r, f_s, f_r, zh_s, zh_r, zl_s, zl_r,
           row_s, row_r, rs0_s, rs0_r, rz_s, rz_r, xa_s, xa_r, fin_s, fin_r):
    r = lax.axis_index("row")
    c = lax.axis_index("col")
    x, zh = r // 2, r % 2
    y, zl, core = c // 8, (c // 2) % 4, c % 2
    me = (y * 2 + core) * 4 + x
    me64 = zh * 32 + me

    def dev(x_, zh_, y_, zl_, core_):
        return (x_ * 2 + zh_, y_ * 8 + zl_ * 2 + core_)

    def dev64(e):
        return dev(e % 4, e // 32, (e // 8) % 4, zl, (e // 4) % 2)

    barrier = pltpu.get_barrier_semaphore()

    def greet_64(i, _):
        pl.semaphore_signal(barrier, inc=1, device_id=dev64((me64 + i) % 64), device_id_type=MESH)
        return 0

    def greet_zl(i, _):
        pl.semaphore_signal(
            barrier, inc=1, device_id=dev(x, zh, (i // 2) % 4, (zl + i // 8) % 4, i % 2),
            device_id_type=MESH)
        return 0

    lax.fori_loop(1, 64, greet_64, 0)
    lax.fori_loop(8, 32, greet_zl, 0)

    def remote(src, dst, ssem, rsem, device):
        return pltpu.make_async_remote_copy(
            src_ref=src, dst_ref=dst, send_sem=ssem, recv_sem=rsem,
            device_id=device, device_id_type=MESH)

    gain0 = norm_in[0:1, :]
    gain1 = norm_in[1:2, :]
    near = dev(x, 1 - zh, y, zl, core)

    sub = lax.broadcasted_iota(jnp.int32, (16, 8, 128), 1)
    none = jnp.zeros((16, 8, 128), F32)

    def weights(d, which):
        for part in range(2):
            at = which * 256 + part * 128
            t = w[d, :, at:at + 128].astype(F32).T.reshape(16, 8, 128)
            turned = pltpu.roll(t, 4, 1)
            even = jnp.concatenate(
                [jnp.where(sub < 4, t, none), jnp.where(sub < 4, none, turned)], axis=2)
            odd = jnp.concatenate(
                [jnp.where(sub < 4, turned, none), jnp.where(sub < 4, none, t)], axis=2)
            both = jnp.concatenate([even[:, None], odd[:, None]], axis=1)
            wb[d, which, part * 256:part * 256 + 256, :] = both.reshape(256, 256).astype(BF)

    weights(0, 0)
    weights(1, 0)
    weights(0, 1)
    weights(1, 1)

    def norm_body(i, _):
        n = WIDE * COLS
        v = pair[pl.ds(i * WIDE, WIDE)].astype(F32).reshape(n, 128)
        xhat[pl.ds(pl.multiple_of(i * n, 8), n), :] = unit_norm(v, 1)
        return 0

    lax.fori_loop(0, ROWS // WIDE, norm_body, 0)

    pad = jnp.zeros((8, 128), F32)

    def band_rows(p):
        rows = []
        for u in (p, p + 16):
            tl = ((u // 2) % 4) * 8 + (u // 8) * 2 + u % 2
            rows += [xhat[tl * 7 * COLS:tl * 7 * COLS + COLS, :] * gain0, pad]
        return jnp.concatenate(rows, axis=0).astype(BF)

    def pairs(a, b):
        return jnp.concatenate([a, b], axis=1)

    def stack(a, b):
        n = a.shape[1]
        return jnp.concatenate([a.reshape(32, 8, n), b.reshape(32, 8, n)], axis=1).astype(BF)

    for i in range(4):
        rows = jnp.concatenate(
            [pairs(band_rows(4 * i), band_rows(4 * i + 1)),
             pairs(band_rows(4 * i + 2), band_rows(4 * i + 3))], axis=0)
        v = gate_value(nt(wb[0, 0], rows))
        f0s[:, i] = stack(v[:, :128], v[:, 128:])

    def column(k, gain):
        return xhat[pl.ds(k, ROWS, stride=COLS), :] * gain

    pad32 = jnp.zeros((32, 256), F32)
    for i in range(2):
        v = []
        for j in range(2):
            b = 4 * i + 2 * j
            rows = pairs(column(7 * b, gain1), column(7 * b + 7, gain1))
            v.append(gate_value(nt(wb[1, 0], jnp.concatenate([rows, pad32], axis=0).astype(BF))))
        f1s[:, i] = stack(v[0], v[1])

    pl.semaphore_wait(barrier, 87)

    def a2a_start(src, dst, ssem, rsem):
        def go(i, _):
            e = (me + i) % 32
            remote(src(e), dst, ssem, rsem, dev(e % 4, zh, e // 8, zl, (e // 4) % 2)).start()
            return 0
        lax.fori_loop(1, 32, go, 0)

    def all_wait(src, dst, ssem, rsem):
        d = remote(src, dst, ssem, rsem, near)
        d.wait_send()
        d.wait_recv()

    a2a_start(lambda e: f0s.at[e], f0r.at[me], f_s.at[0], f_r.at[0])
    f0r[me] = f0s[me]
    a2a_start(lambda e: f1s.at[e], f1r.at[me], f_s.at[1], f_r.at[1])
    f1r[me] = f1s[me]

    def rows_start(i, _):
        cc = (c + i) % 32
        remote(pair.at[cc * 7], grow.at[c], row_s, row_r, (r, cc)).start()
        return 0

    lax.fori_loop(1, 32, rows_start, 0)
    grow[c] = pair[c * 7]

    def second(d, gain, send, recv):
        def group(k):
            low, high = [], []
            for j in range(4):
                v = pairs(column(k * 8 + 2 * j, gain), column(k * 8 + 2 * j + 1, gain))
                low.append(v[:128])
                high.append(v[128:])
            rows = jnp.concatenate(low + high, axis=0).astype(BF)
            v = gate_value(nt(wb[d, 1], rows))
            return [v[:, n * 128:(n + 1) * 128] for n in range(7)]

        for ch, (first, last, t0, t1) in enumerate(CUTS):
            for k in range((last - first) // 2):
                at = t0 + 7 * k
                blocks = group(first + 2 * k) + group(first + 2 * k + 1)
                for n in range(7):
                    send[:, at + n] = stack(blocks[2 * n], blocks[2 * n + 1])
            if (last - first) % 2:
                blocks = group(last - 1)
                blocks.append(jnp.zeros_like(blocks[0]))
                for n in range(4):
                    send[:, t1 - 4 + n] = stack(blocks[2 * n], blocks[2 * n + 1])
            part = pl.ds(t0, t1 - t0)
            a2a_start(lambda e: send.at[e, part], recv.at[me, part], a2a_s.at[d, ch], a2a_r.at[d, ch])
            recv[me, part] = send[me, part]

    def second_wait(d, send, recv):
        for ch, (_, _, t0, t1) in enumerate(CUTS):
            part = pl.ds(t0, t1 - t0)
            all_wait(send.at[pl.ds(0, 31), part], recv.at[pl.ds(0, 31), part],
                     a2a_s.at[d, ch], a2a_r.at[d, ch])

    second(0, gain0, send0, recv0)

    all_wait(f0s.at[pl.ds(0, 31)], f0r.at[pl.ds(0, 31)], f_s.at[0], f_r.at[0])
    for x_ in range(4):
        for y_ in range(4):
            a = f0r[y_ * 8 + x_].astype(F32).reshape(64, 128)
            b = f0r[y_ * 8 + 4 + x_].astype(F32).reshape(64, 128)
            low = lane_of(a) < 64
            tmp[0, 0:64, :] = jnp.where(low, a, roll(b, 64))
            tmp[0, 64:128, :] = jnp.where(low, roll(a, 64), b)
            for h in range(4):
                lhs0[zh, h, x_ * 32:(x_ + 1) * 32, y_ * 128:(y_ + 1) * 128] = (
                    tmp[0, pl.ds(h, 32, stride=4), :].astype(BF))
    zh_copy = remote(lhs0.at[zh], lhs0.at[zh], zh_s, zh_r, near)
    zh_copy.start()

    all_wait(f1s.at[pl.ds(0, 31)], f1r.at[pl.ds(0, 31)], f_s.at[1], f_r.at[1])
    for x_ in range(4):
        for y_ in range(4):
            for half in range(2):
                lanes = slice(half * 128, half * 128 + 128)
                for cc in range(2):
                    tmp[half, cc * 32:cc * 32 + 32, :] = (
                        f1r[y_ * 8 + cc * 4 + x_, :, :, lanes].astype(F32).reshape(32, 128))
                for h in range(4):
                    at = x_ * 256 + half * 128
                    lhs1[zl, h, y_ * 16:(y_ + 1) * 16, at:at + 128] = (
                        tmp[half, pl.ds(h, 16, stride=4), :].astype(BF))
    zl_copies = [remote(lhs1.at[zl], lhs1.at[zl], zl_s.at[i], zl_r.at[i],
                        dev(x, zh, y, (zl + i) % 4, core)) for i in range(1, 4)]
    for d in zl_copies:
        d.start()

    second(1, gain1, send1, recv1)

    all_wait(grow.at[pl.ds(0, 31)], grow.at[pl.ds(0, 31)], row_s, row_r)

    def gates(i, _):
        v = unit_norm(grow[pl.ds(i * 4, 4)].astype(F32).reshape(4 * COLS, 128), 1)
        at = pl.ds(pl.multiple_of(i * 4 * COLS, 8), 4 * COLS)
        g0[at, :] = sigmoid(jnp.dot((v * gain0).astype(BF), gate_w[0], preferred_element_type=F32))
        g1[at, :] = sigmoid(jnp.dot((v * gain1).astype(BF), gate_w[1], preferred_element_type=F32))
        return 0

    lax.fori_loop(0, 8, gates, 0)

    def spread(recv, x_, y_):
        for cc in range(2):
            v = recv[y_ * 8 + cc * 4 + x_].astype(F32).reshape(50, 8, 128)
            for k in range(7):
                at = cc * 224 + k * 32
                n = k * 7
                tmp[0, at:at + 32, :] = v[n:n + 4].reshape(32, 128)
                for j, q in enumerate(unpack(v[n + 4], v[n + 5], v[n + 6])):
                    tmp[1, at + j * 8:at + j * 8 + 8, :] = q

    second_wait(0, send0, recv0)

    def spread0(i, _):
        x_, y_ = i % 4, i // 4
        spread(recv0, x_, y_)
        for h in range(4):
            for half in range(2):
                v = jnp.concatenate(
                    [tmp[half, pl.ds(h, 56, stride=4), :], pad,
                     tmp[half, pl.ds(h + 224, 56, stride=4), :], pad], axis=0)
                rhs0[h * 4 + x_, pl.ds(pl.multiple_of(y_ * 128, 128), 128),
                     half * 128:half * 128 + 128] = v.astype(BF)
        return 0

    lax.fori_loop(0, 16, spread0, 0)
    zh_copy.wait_recv()

    def product0(i, _):
        a = lhs0[:, i // 4].reshape(256, 512)
        v = jnp.dot(a, rhs0[i], preferred_element_type=F32).reshape(8, 4, 8, 256)
        for q in range(4):
            part0[q, i] = v[:, q].reshape(64, 256).astype(BF)
        return 0

    lax.fori_loop(0, 16, product0, 0)
    rs0_copies = [remote(part0.at[(zl + i) % 4], rs0.at[i - 1], rs0_s.at[i], rs0_r.at[i],
                         dev(x, zh, y, (zl + i) % 4, core)) for i in range(1, 4)]
    for d in rs0_copies:
        d.start()

    second_wait(1, send1, recv1)

    def spread1(i, _):
        x_, y_ = i % 4, i // 4
        spread(recv1, x_, y_)
        for h in range(4):
            for half in range(2):
                at = pl.multiple_of(x_ * 256 + half * 128, 128)
                rhs1[h, pl.ds(pl.multiple_of(y_ * 112, 16), 112), pl.ds(at, 128)] = (
                    tmp[half, pl.ds(h, 112, stride=4), :].astype(BF))
        return 0

    lax.fori_loop(0, 16, spread1, 0)
    for d in zl_copies:
        d.wait_recv()

    def product1(h, _):
        a = lhs1[:, h].reshape(256, 1024)
        v = nt(a, rhs1[h]).reshape(2, 2, 4, 16, 448)
        for q in range(2):
            for x_ in range(4):
                part1[q, h, x_ * 32:(x_ + 1) * 32, :] = v[q, :, x_].reshape(32, 448).astype(BF)
        return 0

    lax.fori_loop(0, 4, product1, 0)
    rz = remote(part1.at[1 - zh], zrecv, rz_s, rz_r, near)
    rz.start()

    rz.wait_recv()

    def sum1(h, _):
        v = part1[zh, h].astype(F32) + zrecv[h].astype(F32)
        for x_ in range(4):
            xs[x_, h] = v[x_ * 32:(x_ + 1) * 32].astype(BF)
        return 0

    lax.fori_loop(0, 4, sum1, 0)
    x_copies = [remote(xs.at[(x + i) % 4], xr.at[x], xa_s.at[i], xa_r.at[i],
                       dev((x + i) % 4, zh, y, zl, core)) for i in range(1, 4)]
    for d in x_copies:
        d.start()
    xr[x] = xs[x]

    for d in rs0_copies:
        d.wait_recv()

    def sum0(h, _):
        v = part0[zl, h].astype(F32)
        for i in range(3):
            v = v + rs0[i, h].astype(F32)
        at = pl.ds(pl.multiple_of(h * 64, 64), 64)
        tmp[0, at, :] = v[:, :128]
        tmp[1, at, :] = v[:, 128:]
        return 0

    lax.fori_loop(0, 16, sum0, 0)

    def turn0(t, _):
        fin0s[t] = jnp.concatenate(
            [tmp[half, pl.ds(t, 16, stride=64), :] for half in range(2)], axis=1).astype(BF)
        return 0

    lax.fori_loop(0, 64, turn0, 0)

    def row64(e):
        return (e // 32) * 32 + (e % 4) * 8 + (e // 4) % 8

    def fin0_start(i, _):
        e = (me64 + i) % 64
        remote(fin0s.at[row64(e)], fin0r.at[me64], fin_s.at[0], fin_r.at[0], dev64(e)).start()
        return 0

    lax.fori_loop(1, 64, fin0_start, 0)
    fin0r[me64] = fin0s[row64(me64)]

    for d in x_copies:
        d.wait_recv()

    def fill1(h, _):
        v = xr[h // 4, h % 4].astype(F32)
        for q in range(4):
            part = v[:, q * 128:(q + 1) * 128] if q < 3 else jnp.concatenate(
                [v[:, 384:], jnp.zeros((32, 64), F32)], axis=1)
            tmp[q // 2, pl.ds(pl.multiple_of((q % 2) * 512 + h * 32, 32), 32), :] = part
        return 0

    lax.fori_loop(0, 16, fill1, 0)

    def turn1(t, _):
        v = jnp.concatenate(
            [tmp[q // 2, pl.ds((q % 2) * 512 + t, 16, stride=32), :] for q in range(4)], axis=1)
        fin1s[t] = v[:, :448].astype(BF)
        return 0

    lax.fori_loop(0, 32, turn1, 0)

    def fin1_start(i, _):
        cc = (c + i) % 32
        remote(fin1s.at[cc], fin1r.at[c], fin_s.at[1], fin_r.at[1], (r, cc)).start()
        return 0

    lax.fori_loop(1, 32, fin1_start, 0)
    fin1r[c] = fin1s[c]

    all_wait(fin0s.at[pl.ds(0, 63)], fin0r.at[pl.ds(0, 63)], fin_s.at[0], fin_r.at[0])

    def settle(v, d):
        return (unit_norm(v, 0) * norm_out[d]).astype(BF)

    for z_ in range(2):
        v = fin0r[z_ * 32:z_ * 32 + 32].astype(F32).reshape(512, 256)
        tmp[0, 0:512, :] = v[:, :128]
        tmp[1, 0:512, :] = v[:, 128:]
        for x_ in range(4):
            v = jnp.concatenate([tmp[half, pl.ds(x_, 128, stride=4), :] for half in range(2)], axis=1)
            linear = tn(settle(v, 0), out_w[0])[:ROWS]
            at = (x_ * 2 + z_) * ROWS
            out0[0, at:at + ROWS, :] = (g0[at:at + ROWS, :] * linear).astype(BF)

    all_wait(fin1s.at[pl.ds(0, 31)], fin1r.at[pl.ds(0, 31)], fin_s.at[1], fin_r.at[1])
    for z_ in range(4):
        v = jnp.concatenate(
            [fin1r[y_ * 8 + z_ * 2 + cc] for y_ in range(4) for cc in range(2)], axis=0)
        linear = tn(settle(v.astype(F32), 1), out_w[1])
        for y_ in range(4):
            at = (y_ * 8 + z_ * 2) * COLS
            out1[0, at:at + 112, :] = (
                g1[at:at + 112, :] * linear[y_ * 112:(y_ + 1) * 112]).astype(BF)

    zh_copy.wait_send()
    rz.wait_send()
    for d in zl_copies + rs0_copies + x_copies:
        d.wait_send()


def shards(pair_rep, norm_in, proj_weight, gate_weight, norm_out, out_weight):
    vm = pl.BlockSpec(memory_space=pltpu.VMEM)
    dma = pltpu.SemaphoreType.DMA
    V = pltpu.VMEM
    return pl.pallas_call(
        kernel,
        name="triangles",
        out_shape=[jax.ShapeDtypeStruct((1, 1792, 128), BF)] * 2,
        in_specs=[vm] * 6,
        out_specs=[vm] * 2,
        scratch_shapes=[
            V((ROWS * COLS, 128), F32), V((2, 2, 512, 256), BF),
            V((32, TILES, 16, 128), BF), V((32, TILES, 16, 128), BF),
            V((32, TILES, 16, 128), BF), V((32, TILES, 16, 128), BF),
            V((32, 4, 16, 128), BF), V((32, 4, 16, 128), BF),
            V((32, 2, 16, 256), BF), V((32, 2, 16, 256), BF),
            V((2, 4, 128, 512), BF), V((4, 4, 64, 1024), BF),
            V((16, 512, 256), BF), V((4, 448, 1024), BF),
            V((2, 1024, 128), F32),
            V((4, 16, 64, 256), BF), V((3, 16, 64, 256), BF),
            V((2, 4, 128, 448), BF), V((4, 128, 448), BF),
            V((4, 4, 32, 448), BF), V((4, 4, 32, 448), BF),
            V((64, 16, 256), BF), V((64, 16, 256), BF),
            V((32, 16, 448), BF), V((32, 16, 448), BF),
            V((32, COLS, 128), BF), V((1792, 128), F32), V((1792, 128), F32),
            dma((2, 2)), dma((2, 2)), dma((2,)), dma((2,)), dma, dma,
            dma((4,)), dma((4,)), dma, dma, dma((4,)), dma((4,)), dma, dma,
            dma((4,)), dma((4,)), dma((2,)), dma((2,)),
        ],
        compiler_params=pltpu.CompilerParams(
            collective_id=0, has_side_effects=True, vmem_limit_bytes=60 << 20),
    )(pair_rep, norm_in, proj_weight, gate_weight, norm_out[:, :, None], out_weight)


def solution(mesh):
    in_specs = (P("row", "col", None), P(), P(), P(), P(), P())
    out_specs = (P(("row", "col"), None, None), P(("row", "col"), None, None))
    return jax.shard_map(shards, mesh=mesh, in_specs=in_specs, out_specs=out_specs, check_vma=False)
```

time: 553 us -> 230 us (0.42)
  the two profiles are of different devices: /device:TPU:1 before, /device:TPU:197 now
where the time goes in v2:
time: 230 us
  Pallas kernels  224 us (97%)
  local copies, waits for them, and re-layouts  5.1 us (2%)
    pallas_call x1, Pallas kernels, shards(): pl.pallas_call(kernel, name='triangles', out_shape=[jax.ShapeDtypeStruct(...  224 us

profile of v2, /device:TPU:197, one launch (start us, length us, event | category | flops | bytes accessed | tf_op | source)
XLA Modules:
  0.0 229.6 jit_solution(7422528593132534328)
XLA Ops:
  0.6 1.5 copy.8.norm_out
  2.1 223.9 %triangles.1 = (bf16[1,1792,128]{2,1,0:T(8,128)(2,1)}, bf16[1,1792,128]{2,1,0:T(8,128)(2,1)}) custom-call(bf16[224,56,128]{2,1,0:T(8,128)(2,1)} %pair.1, f32[2,128]{1,0:T(2,128)} %norm_in.1, bf16[2,128,512]{2,1,0:T(8,128)(2,1)} %w.1, bf16[2,128,128]{2,1,0:T(8,128)(2,1)} %gate_w.1, f32[2,128,1]{2,1,0:T(8,128)} %copy.8.norm_out, bf16[2,128,128]{2,1,0:T(8,128)(2,1)} %out_w.1), custom_call_target="tpu_custom_call" | custom-call | tf_op jit(solution)/shard_map/triangles/pallas_call | solution.py:450
  226.0 1.8 copy.11
  227.8 1.8 copy.12
